TPU v7x, 256 devices: a whole 4x4x8 slice. The times are simulated.
256 devices in a mesh: replica: 32 (over x, z), shard: 8 (over y, core).
Axes of the slice: x: 4, y: 4, z: 8, core: 2. Of those that a mesh axis runs over, the one named last changes fastest.
Arguments:
- grads: bfloat16 [32, 8192, 2048], P('replica', 'shard'), may hold values from -64 to 64
- errors: bfloat16 [32, 8192, 2048], P('replica', 'shard'), may hold values from -4 to 4
- q_prev: bfloat16 [32, 2048], P(None, 'shard'), may hold values from -6 to 6
- momentum: float32 [8192, 2048], P('shard', 'replica'), may hold values from -1.2 to 1.2
Outputs:
- new_errors: bfloat16 [32, 8192, 2048], P('replica', 'shard')
- new_momentum: float32 [8192, 2048], P('shard', 'replica')
- q_next: float32 [32, 2048], P(None, 'shard')
All inputs are finite; a program needn't handle non-finite values.
Results may differ from a plain program's by a relative error of at most 0.012.
Values may be sent and summed in bfloat16 or wider, within the bound.
A program may use at most 64 MiB of HBM per device.

v0:
```python
import jax
import jax.numpy as jnp
from jax import lax
from jax.sharding import PartitionSpec as P


def shards(grads, errors, q_prev, momentum):
    highest = lax.Precision.HIGHEST
    merged = grads[0].astype(jnp.float32) + errors[0].astype(jnp.float32)
    col_count = merged.shape[1]
    product = lax.dot_general(
        merged,
        lax.all_gather(q_prev, "shard", axis=1, tiled=True).astype(jnp.float32),
        (((1,), (1,)), ((), ())),
        precision=highest,
    )
    factor = lax.psum(product.astype(jnp.bfloat16), "replica").astype(jnp.float32)
    every_row = lax.all_gather(factor.astype(jnp.bfloat16), "shard", axis=0, tiled=True).astype(
        factor.dtype
    )
    gram_matrix = jnp.dot(every_row.T, every_row, precision=highest)
    lower_factor = jnp.linalg.cholesky(gram_matrix)
    ortho = jax.scipy.linalg.solve_triangular(lower_factor, factor.T, lower=True).T
    right_term = jnp.dot(ortho.T, merged, precision=highest)
    replicas = lax.axis_size("replica")
    block_width = col_count // lax.axis_size("shard")
    right_full = lax.psum(right_term, ("replica", "shard")) / replicas
    q_next = lax.dynamic_slice_in_dim(
        right_full, lax.axis_index("shard") * block_width, block_width, 1
    )
    approx = jnp.dot(ortho, right_full, precision=highest)
    new_errors = (merged - approx).astype(jnp.bfloat16)[None]
    momentum_width = momentum.shape[1]
    approx_block = lax.dynamic_slice_in_dim(
        approx, lax.axis_index("replica") * momentum_width, momentum_width, 1
    )
    new_momentum = 0.9 * momentum + approx_block
    return (new_errors, new_momentum, q_next)


def solution(mesh):
    return jax.shard_map(
        shards,
        mesh=mesh,
        in_specs=(
            P("replica", "shard", None),
            P("replica", "shard", None),
            P(None, "shard"),
            P("shard", "replica"),
        ),
        out_specs=(P("replica", "shard", None), P("shard", "replica"), P(None, "shard")),
        check_vma=False,
    )
```

profile of v0, /device:TPU:2, one launch (start us, length us, event | category | flops | bytes accessed | tf_op | source)
XLA Modules:
  0.0 478.8 jit_solution(6031099820396762904)
XLA Ops:
  7.2 0.0 all-reduce.3.cloned.1.call-start
  7.2 13.5 %all_gather.6 = bf16[32,2048]{1,0:T(8,128)(2,1)S(1)} all-gather(bf16[32,256]{1,0:T(8,128)(2,1)} %param.6), channel_id=1, replica_groups=mesh['replica'=32,'shard'=8] {'shard'}, dimensions={1}, use_global_device_ids=true | all-gather | bytes 147456 | tf_op jit(solution)/shard_map/all_gather | solution.py:13
  20.7 0.0 copy-start.2
  20.7 9.1 %fusion.6 = bf16[1024,32]{0,1:T(8,128)(2,1)} fusion(bf16[32,2048]{1,0:T(8,128)(2,1)S(1)} %all_gather.6, bf16[1,1024,2048]{2,1,0:T(8,128)(2,1)} %param.5, bf16[1,1024,2048]{2,1,0:T(8,128)(2,1)} %param.4), kind=kOutput, calls=%fused_computation.8 | convolution fusion | flops 811630592 | bytes 8585216 | tf_op jit(solution)/shard_map/dot_general | solution.py:11
  29.8 0.0 all-reduce.3.cloned.1.call-update
  29.8 0.0 all-reduce.5.cloned.1.call-start
  29.8 141.3 %all-reduce.3.cloned.1.call-done = bf16[1024,32]{0,1:T(8,128)(2,1)} async-done(((bf16[1024,32]{0,1:T(8,128)(2,1)}), bf16[1024,32]{0,1:T(8,128)(2,1)}) %all-reduce.3.cloned.1.call-update) | async-done | bytes 65552 | tf_op jit(solution)/shard_map/psum | solution.py:17
  171.2 13.8 %all_gather.7 = bf16[8192,32]{0,1:T(8,128)(2,1)S(1)} all-gather(bf16[1024,32]{0,1:T(8,128)(2,1)} %all-reduce.3.cloned.1.call-done), channel_id=1, replica_groups=mesh['replica'=32,'shard'=8] {'shard'}, dimensions={0}, use_global_device_ids=true | all-gather | bytes 589824 | tf_op jit(solution)/shard_map/all_gather | solution.py:18
  185.0 0.3 fusion.14
  185.3 0.1 copy.7
  185.4 2.9 cholesky.16
  188.3 0.6 compare_reduce_fusion
  189.0 0.7 fusion.9
  189.6 2.4 custom-call.7
  192.1 1.1 fusion.10
  193.2 8.6 %fusion = f32[32,2048]{1,0:T(8,128)} fusion(f32[32,1024]{1,0:T(8,128)S(1)} %fusion.10, bf16[1,1024,2048]{2,1,0:T(8,128)(2,1)} %param.5, bf16[1,1024,2048]{2,1,0:T(8,128)(2,1)} %param.4), kind=kOutput, calls=%fused_computation.1 | convolution fusion | flops 811597824 | bytes 8781824 | tf_op jit(solution)/shard_map/dot_general | solution.py:24
  201.7 0.0 all-reduce.5.cloned.1.call-update
  201.8 0.0 copy-done.2
  201.8 0.2 copy.8
  202.0 248.0 %all-reduce.5.cloned.1.call-done = f32[32,2048]{1,0:T(8,128)} async-done(((f32[32,2048]{1,0:T(8,128)}), f32[32,2048]{1,0:T(8,128)}) %all-reduce.5.cloned.1.call-update) | async-done | bytes 262160 | tf_op jit(solution)/shard_map/psum | solution.py:27
  450.0 0.0 copy-start
  450.0 10.0 %fusion.13 = f32[1024,2048]{1,0:T(8,128)} fusion(f32[32,1024]{1,0:T(8,128)S(1)} %fusion.10, f32[32,2048]{1,0:T(8,128)} %all-reduce.5.cloned.1.call-done), kind=kOutput, calls=%fused_computation.22 | convolution fusion | flops 805371904 | bytes 8781824 | tf_op jit(solution)/shard_map/dot_general | solution.py:31
  459.9 0.0 copy-done
  459.9 0.0 copy-start.1
  459.9 9.2 %fusion.5 = bf16[1,1024,2048]{2,1,0:T(8,128)(2,1)} fusion(f32[1024,2048]{1,0:T(8,128)} %fusion.13, bf16[1,1024,2048]{2,1,0:T(8,128)(2,1)S(1)} %copy-done, bf16[1,1024,2048]{2,1,0:T(8,128)(2,1)} %param.4), kind=kLoop, calls=%fused_computation.7 | loop fusion | flops 10485760 | bytes 20971520 | tf_op jit(solution)/shard_map/broadcast_in_dim | solution.py:32
  469.2 1.2 dynamic-slice_add_fusion
  470.4 0.9 copy.9
  471.3 0.0 copy-done.1
  471.3 0.6 constant_dynamic-slice_fusion
  (3 shorter events, 0.1 us)
Async XLA Ops:
  7.2 164.0 %all-reduce.3.cloned.1.call-start = ((), (), s32[]{:S(2)}) async-start(), calls=%async_computation | async-start | bytes 131072 | tf_op jit(solution)/shard_map/psum | solution.py:17
  20.7 181.1 %copy-start.2 = (f32[1024,64]{0,1:T(8,128)S(1)}, f32[1024,64]{0,1:T(8,128)}, u32[]{:S(2)}) copy-start(f32[1024,64]{0,1:T(8,128)} %param.7) | copy-start | bytes 786436
  29.8 420.2 %all-reduce.5.cloned.1.call-start = ((), (), s32[]{:S(2)}) async-start(), calls=%async_computation.1 | async-start | bytes 524288 | tf_op jit(solution)/shard_map/psum | solution.py:27
  450.0 10.0 %copy-start = (bf16[1,1024,2048]{2,1,0:T(8,128)(2,1)S(1)}, bf16[1,1024,2048]{2,1,0:T(8,128)(2,1)}, u32[]{:S(2)}) copy-start(bf16[1,1024,2048]{2,1,0:T(8,128)(2,1)} %param.5) | copy-start | bytes 12582916
  459.9 11.4 %copy-start.1 = (f32[32,2048]{1,0:T(8,128)S(1)}, f32[32,2048]{1,0:T(8,128)}, u32[]{:S(2)}) copy-start(f32[32,2048]{1,0:T(8,128)} %all-reduce.5.cloned.1.call-done) | copy-start | bytes 786436
Sparse Core Ops, SparseCore 0:
  29.9 141.2 all-reduce.2
  201.9 248.0 all-reduce.4
where the time goes:
time: 479 us
  waiting for transfers between devices  389 us (81%)
  matrix products  29 us (6%)
  blocking collectives  27.3 us (6%)
  other arithmetic  17.2 us (4%)
  between operations  14.1 us (3%)
    psum x1, waiting for transfers between devices, shards(): right_full = lax.psum(right_term, ('replica', 'shard')) / replicas  248 us
    psum x1, waiting for transfers between devices, shards(): lax.psum(product.astype(jnp.bfloat16), 'replica').astype(jnp.float32)  141 us
    all_gather x1, blocking collectives, shards(): lax.all_gather(factor.astype(jnp.bfloat16), 'shard', axis=0, tiled=True)  13.8 us
    all_gather x1, blocking collectives, shards(): lax.all_gather(q_prev, 'shard', axis=1, tiled=True).astype(jnp.float32)  13.5 us
    dot_general x1, matrix products, shards(): approx = jnp.dot(ortho, right_full, precision=highest)  9.98 us
  transfers between devices with their start and end apart: 2, of which 2 were waited for; matrix products, arithmetic and copies ran while one was open for 0% of the time, Pallas kernels for 0%

commit v1 on v0

--- a/solution.py
+++ b/solution.py
@@ -2,6 +2,11 @@
 import jax.numpy as jnp
 from jax import lax
 from jax.sharding import PartitionSpec as P
+
+
+def axis_by_axis(value, inner_axis, outer_axis):
+    inner = lax.psum(value, inner_axis)
+    return lax.psum(inner, outer_axis)
 
 
 def shards(grads, errors, q_prev, momentum):
@@ -24,7 +29,7 @@
     right_term = jnp.dot(ortho.T, merged, precision=highest)
     replicas = lax.axis_size("replica")
     block_width = col_count // lax.axis_size("shard")
-    right_full = lax.psum(right_term, ("replica", "shard")) / replicas
+    right_full = axis_by_axis(right_term, "shard", "replica") / replicas
     q_next = lax.dynamic_slice_in_dim(
         right_full, lax.axis_index("shard") * block_width, block_width, 1
     )

time: 479 us -> 440 us (0.919)
  waiting for transfers between devices: 389 us -> 350 us
    psum x1 -> x2, waiting for transfers between devices: 248 us -> 208 us  [the longest x1 146 us: axis_by_axis(): return lax.psum(inner, outer_axis)]
  transfers between devices with their start and end apart: 2 -> 3, of which waited for: 2 -> 3; matrix products, arithmetic and copies ran while one was open for 0% -> 0% of each run, Pallas kernels for 0% -> 0%
where the time goes in v1:
time: 440 us; the launch traced here: 439 us
  waiting for transfers between devices  350 us (80%)
  matrix products  29 us (7%)
  blocking collectives  27.1 us (6%)
  other arithmetic  17.2 us (4%)
  between operations  13.8 us (3%)
    psum x1, waiting for transfers between devices, axis_by_axis(): return lax.psum(inner, outer_axis)  146 us
    psum x1, waiting for transfers between devices, shards(): lax.psum(product.astype(jnp.bfloat16), 'replica').astype(jnp.float32)  141 us
    psum x1, waiting for transfers between devices, axis_by_axis(): inner = lax.psum(value, inner_axis)  62.7 us
    all_gather x1, blocking collectives, shards(): lax.all_gather(factor.astype(jnp.bfloat16), 'shard', axis=0, tiled=True)  13.6 us
    all_gather x1, blocking collectives, shards(): lax.all_gather(q_prev, 'shard', axis=1, tiled=True).astype(jnp.float32)  13.5 us
    dot_general x1, matrix products, shards(): approx = jnp.dot(ortho, right_full, precision=highest)  9.98 us
    broadcast_in_dim x1, other arithmetic, shards(): new_errors = (merged - approx).astype(jnp.bfloat16)[None]  9.22 us
    dot_general x1, matrix products, shards(): lax.dot_general(merged, lax.all_gather(q_prev, 'shard', axis=1, tiled=Tru...  9.05 us
  transfers between devices with their start and end apart: 3, of which 3 were waited for; matrix products, arithmetic and copies ran while one was open for 0% of the time, Pallas kernels for 0%

profile of v1, /device:TPU:2, one launch (start us, length us, event | category | flops | bytes accessed | tf_op | source)
XLA Modules:
  0.0 438.9 jit_solution(9595012559058689329)
XLA Ops:
  7.2 0.0 all-reduce.4.cloned.1.call-start
  7.2 13.5 %all_gather.6 = bf16[32,2048]{1,0:T(8,128)(2,1)S(1)} all-gather(bf16[32,256]{1,0:T(8,128)(2,1)} %param.6), channel_id=1, replica_groups=mesh['replica'=32,'shard'=8] {'shard'}, dimensions={1}, use_global_device_ids=true | all-gather | bytes 147456 | tf_op jit(solution)/shard_map/all_gather | solution.py:18
  20.7 0.0 copy-start.2
  20.7 9.1 %fusion.6 = bf16[1024,32]{0,1:T(8,128)(2,1)} fusion(bf16[32,2048]{1,0:T(8,128)(2,1)S(1)} %all_gather.6, bf16[1,1024,2048]{2,1,0:T(8,128)(2,1)} %param.5, bf16[1,1024,2048]{2,1,0:T(8,128)(2,1)} %param.4), kind=kOutput, calls=%fused_computation.8 | convolution fusion | flops 811630592 | bytes 8585216 | tf_op jit(solution)/shard_map/dot_general | solution.py:16
  29.8 0.0 all-reduce.4.cloned.1.call-update
  29.8 0.0 all-reduce.6.cloned.1.call-start
  29.8 141.3 %all-reduce.4.cloned.1.call-done = bf16[1024,32]{0,1:T(8,128)(2,1)} async-done(((bf16[1024,32]{0,1:T(8,128)(2,1)}), bf16[1024,32]{0,1:T(8,128)(2,1)}) %all-reduce.4.cloned.1.call-update) | async-done | bytes 65552 | tf_op jit(solution)/shard_map/psum | solution.py:22
  171.2 13.6 %all_gather.7 = bf16[8192,32]{0,1:T(8,128)(2,1)S(1)} all-gather(bf16[1024,32]{0,1:T(8,128)(2,1)} %all-reduce.4.cloned.1.call-done), channel_id=1, replica_groups=mesh['replica'=32,'shard'=8] {'shard'}, dimensions={0}, use_global_device_ids=true | all-gather | bytes 589824 | tf_op jit(solution)/shard_map/all_gather | solution.py:23
  184.8 0.3 fusion.14
  185.1 0.1 copy.7
  185.2 2.9 cholesky.16
  188.1 0.6 compare_reduce_fusion
  188.8 0.7 fusion.9
  189.4 2.4 custom-call.7
  191.9 1.1 fusion.10
  193.0 8.6 %fusion = f32[32,2048]{1,0:T(8,128)} fusion(f32[32,1024]{1,0:T(8,128)S(1)} %fusion.10, bf16[1,1024,2048]{2,1,0:T(8,128)(2,1)} %param.5, bf16[1,1024,2048]{2,1,0:T(8,128)(2,1)} %param.4), kind=kOutput, calls=%fused_computation.1 | convolution fusion | flops 811597824 | bytes 8781824 | tf_op jit(solution)/shard_map/dot_general | solution.py:29
  201.6 0.0 all-reduce.6.cloned.1.call-update
  201.6 0.2 all-reduce.8.cloned.1.call-start
  201.8 62.7 %all-reduce.6.cloned.1.call-done = f32[32,2048]{1,0:T(8,128)} async-done(((f32[32,2048]{1,0:T(8,128)}), f32[32,2048]{1,0:T(8,128)}) %all-reduce.6.cloned.1.call-update) | async-done | bytes 262160 | tf_op jit(solution)/shard_map/psum | solution.py:8
  264.5 0.0 all-reduce.8.cloned.1.call-update
  264.5 0.0 copy-done.2
  264.5 0.2 copy.8
  264.7 145.7 %all-reduce.8.cloned.1.call-done = f32[32,2048]{1,0:T(8,128)} async-done(((f32[32,2048]{1,0:T(8,128)}), f32[32,2048]{1,0:T(8,128)}) %all-reduce.8.cloned.1.call-update) | async-done | bytes 262160 | tf_op jit(solution)/shard_map/psum | solution.py:9
  410.4 0.0 copy-start
  410.4 10.0 %fusion.13 = f32[1024,2048]{1,0:T(8,128)} fusion(f32[32,1024]{1,0:T(8,128)S(1)} %fusion.10, f32[32,2048]{1,0:T(8,128)} %all-reduce.8.cloned.1.call-done), kind=kOutput, calls=%fused_computation.22 | convolution fusion | flops 805371904 | bytes 8781824 | tf_op jit(solution)/shard_map/dot_general | solution.py:36
  420.4 0.0 copy-done
  420.4 0.0 copy-start.1
  420.4 9.2 %fusion.5 = bf16[1,1024,2048]{2,1,0:T(8,128)(2,1)} fusion(f32[1024,2048]{1,0:T(8,128)} %fusion.13, bf16[1,1024,2048]{2,1,0:T(8,128)(2,1)S(1)} %copy-done, bf16[1,1024,2048]{2,1,0:T(8,128)(2,1)} %param.4), kind=kLoop, calls=%fused_computation.7 | loop fusion | flops 10485760 | bytes 20971520 | tf_op jit(solution)/shard_map/broadcast_in_dim | solution.py:37
  429.6 1.2 dynamic-slice_add_fusion
  430.8 0.9 copy.9
  431.7 0.0 copy-done.1
  431.7 0.6 constant_dynamic-slice_fusion
  (3 shorter events, 0.1 us)
Async XLA Ops:
  7.2 164.0 %all-reduce.4.cloned.1.call-start = ((), (), s32[]{:S(2)}) async-start(), calls=%async_computation | async-start | bytes 131072 | tf_op jit(solution)/shard_map/psum | solution.py:22
  20.7 243.8 %copy-start.2 = (f32[1024,64]{0,1:T(8,128)S(1)}, f32[1024,64]{0,1:T(8,128)}, u32[]{:S(2)}) copy-start(f32[1024,64]{0,1:T(8,128)} %param.7) | copy-start | bytes 786436
  29.8 234.7 %all-reduce.6.cloned.1.call-start = ((), (), s32[]{:S(2)}) async-start(), calls=%async_computation.1 | async-start | bytes 524288 | tf_op jit(solution)/shard_map/psum | solution.py:8
  201.6 208.8 %all-reduce.8.cloned.1.call-start = ((), (), s32[]{:S(2)}) async-start(), calls=%async_computation.2 | async-start | bytes 524288 | tf_op jit(solution)/shard_map/psum | solution.py:9
  410.4 10.0 %copy-start = (bf16[1,1024,2048]{2,1,0:T(8,128)(2,1)S(1)}, bf16[1,1024,2048]{2,1,0:T(8,128)(2,1)}, u32[]{:S(2)}) copy-start(bf16[1,1024,2048]{2,1,0:T(8,128)(2,1)} %param.5) | copy-start | bytes 12582916
  420.4 11.4 %copy-start.1 = (f32[32,2048]{1,0:T(8,128)S(1)}, f32[32,2048]{1,0:T(8,128)}, u32[]{:S(2)}) copy-start(f32[32,2048]{1,0:T(8,128)} %all-reduce.8.cloned.1.call-done) | copy-start | bytes 786436
Sparse Core Ops, SparseCore 0:
  29.9 141.2 all-reduce.3
  201.7 62.7 all-reduce.5
  268.3 142.0 all-reduce.7
